TPU v7x, 32 devices: a whole 2x2x4 slice. The times are simulated.
32 devices in a mesh: groups: 2 (over x), rows: 16 (over z, y, core).
Axes of the slice: x: 2, y: 2, z: 4, core: 2. Of those that a mesh axis runs over, the one named last changes fastest.
Arguments:
- latent: bfloat16 [128, 256, 384], P(('groups', 'rows')), parts along dimension 0, may hold values from -6 to 6
- cache_frames: bfloat16 [2, 128, 256, 384], P(None, ('groups', 'rows')), parts along dimension 1, may hold values from -6 to 6
- norm_gain: float32 [384], replicated, may hold values from 0.1 to 1.9
- kernel: bfloat16 [3, 3, 3, 384, 384], replicated, may hold values from -0.0625 to 0.0625
- kernel_bias: float32 [384], replicated, may hold values from -3 to 3
Outputs:
- decoded: bfloat16 [128, 256, 384], P(('groups', 'rows')), parts along dimension 0
- next_cache: bfloat16 [128, 256, 384], P(('groups', 'rows')), parts along dimension 0
There are 2 independent parts, one for each index of `groups`. A program takes and returns all parts, laid end to end along the dimension named above; an argument that names none is the same for every part. Nothing has to cross between parts.
All inputs are finite; a program needn't handle non-finite values.
Results may differ from a plain program's by a relative error of at most 0.0021.
Values may be sent and summed in bfloat16 or wider, within the bound.
A program may use at most 128 MiB of HBM per device.

v0:
```python
import jax
import jax.numpy as jnp
from jax import lax
from jax.sharding import PartitionSpec as P

epsilon = 1e-06


def extended(block, sides, width):
    for axis, dim in sides:
        count = lax.axis_size(axis)
        forward = [(i, i + 1) for i in range(count - 1)]
        backward = [(target, source) for source, target in forward]
        low = lax.ppermute(
            lax.slice_in_dim(block, block.shape[dim] - width, None, axis=dim), axis, forward
        )
        high = lax.ppermute(lax.slice_in_dim(block, 0, width, axis=dim), axis, backward)
        block = jnp.concatenate([low, block, high], axis=dim)
    return block


def activate(values, gain):
    values = values.astype(jnp.float32)
    scaled = values * lax.rsqrt(jnp.mean(values * values, axis=-1, keepdims=True) + epsilon) * gain
    return jax.nn.silu(scaled).astype(jnp.bfloat16)


def tap_products(frames, weight):
    out_rows = frames.shape[1] - 2
    out_cols = frames.shape[2] - 2
    channels = frames.shape[3]
    out_width = weight.shape[4]
    running = jnp.zeros((out_rows * out_cols, out_width), jnp.float32)
    for tap_time in range(3):
        for tap_row in range(3):
            for tap_col in range(3):
                window = frames[
                    tap_time, tap_row : tap_row + out_rows, tap_col : tap_col + out_cols, :
                ]
                running = running + jnp.dot(
                    window.reshape(out_rows * out_cols, channels),
                    weight[tap_time, tap_row, tap_col],
                    preferred_element_type=jnp.float32,
                )
    return running.reshape(out_rows, out_cols, out_width)


def on_device(latent, cache_frames, norm_gain, kernel, kernel_bias):
    cache_ext = extended(cache_frames, (("rows", 1),), 1)
    next_cache = activate(latent, norm_gain)
    frame_ext = extended(next_cache, (("rows", 0),), 1)
    frames = jnp.concatenate([cache_ext, frame_ext[None]], axis=0)
    padded = jnp.pad(frames, ((0, 0), (0, 0), (1, 1), (0, 0)))
    branch = tap_products(padded, kernel) + kernel_bias
    decoded = (latent.astype(jnp.float32) + branch).astype(jnp.bfloat16)
    return (decoded, next_cache)


def solution(mesh):
    in_specs = (
        P(("groups", "rows"), None, None),
        P(None, ("groups", "rows"), None, None),
        P(),
        P(),
        P(),
    )
    out_specs = (P(("groups", "rows"), None, None), P(("groups", "rows"), None, None))
    return jax.shard_map(
        on_device, mesh=mesh, in_specs=in_specs, out_specs=out_specs, check_vma=False
    )
```

profile of v0, /device:TPU:24, one launch (start us, length us, event | category | flops | bytes accessed | tf_op | source)
XLA Modules:
  0.0 89.3 jit_solution(12832361347385717654)
XLA Ops:
  0.6 1.5 %fusion.4 = f32[4,256]{1,0:T(4,128)S(1)} fusion(bf16[4,256,384]{2,1,0:T(8,128)(2,1)} %param.5), kind=kLoop, calls=%fused_computation.11 | loop fusion | flops 1178624 | bytes 790528 | tf_op jit(solution)/shard_map/reduce_sum | solution.py:24
  2.1 1.7 %fusion.11 = bf16[4,256,384]{2,1,0:T(8,128)(2,1)S(1)} fusion(bf16[4,256,384]{2,1,0:T(8,128)(2,1)} %param.5, f32[384]{0:T(512)} %param.7, f32[4,256]{1,0:T(4,128)S(1)} %add_rsqrt_fusion), kind=kLoop, calls=%fused_computation.18 | loop fusion | flops 3145728 | bytes 1578496 | tf_op jit(solution)/shard_map/convert_element_type | solution.py:25
  3.8 0.0 copy-start.3
  3.8 0.0 copy-start.1
  3.9 2.3 %collective-permute-start.2 = (bf16[1,256,384]{2,1,0:T(8,128)(2,1)S(1)}, bf16[1,256,384]{2,1,0:T(8,128)(2,1)S(1)}, u32[]{:S(2)}, u32[]{:S(2)}) collective-permute-start(bf16[1,256,384]{2,1,0:T(8,128)(2,1)S(1)} %get-tuple-element.33), channel_id=1, source_target_pairs={{0,1},{1,2},{2,3},{3,4},{4,5},{5,6},{6,7},{7,8},{8,9},{9,10},{10,1... | collective-permute-start | bytes 589832 | tf_op jit(solution)/shard_map/ppermute | solution.py:14
  6.2 4.4 %collective-permute-start.3 = (bf16[1,256,384]{2,1,0:T(8,128)(2,1)S(1)}, bf16[1,256,384]{2,1,0:T(8,128)(2,1)S(1)}, u32[]{:S(2)}, u32[]{:S(2)}) collective-permute-start(bf16[1,256,384]{2,1,0:T(8,128)(2,1)S(1)} %get-tuple-element.34), channel_id=1, source_target_pairs={{1,0},{2,1},{3,2},{4,3},{5,4},{6,5},{7,6},{8,7},{9,8},{10,9},{11,1... | collective-permute-start | bytes 589832 | tf_op jit(solution)/shard_map/ppermute | solution.py:17
  10.6 0.1 fusion.97
  10.7 1.9 %collective-permute-start = (bf16[2,1,256,384]{3,2,1,0:T(8,128)(2,1)S(1)}, bf16[2,1,256,384]{3,2,1,0:T(8,128)(2,1)S(1)}, u32[]{:S(2)}, u32[]{:S(2)}) collective-permute-start(bf16[2,1,256,384]{3,2,1,0:T(8,128)(2,1)S(1)} %get-tuple-element.28), channel_id=1, source_target_pairs={{0,1},{1,2},{2,3},{3,4},{4,5},{5,6},{6,7},{7,8},{8,9},{9,10},{10,1... | collective-permute-start | bytes 1179656 | tf_op jit(solution)/shard_map/ppermute | solution.py:14
  12.6 4.5 %collective-permute-start.1 = (bf16[2,1,256,384]{3,2,1,0:T(8,128)(2,1)S(1)}, bf16[2,1,256,384]{3,2,1,0:T(8,128)(2,1)S(1)}, u32[]{:S(2)}, u32[]{:S(2)}) collective-permute-start(bf16[2,1,256,384]{3,2,1,0:T(8,128)(2,1)S(1)} %get-tuple-element.29), channel_id=1, source_target_pairs={{1,0},{2,1},{3,2},{4,3},{5,4},{6,5},{7,6},{8,7},{9,8},{10,9},{11,1... | collective-permute-start | bytes 1179656 | tf_op jit(solution)/shard_map/ppermute | solution.py:17
  17.2 0.2 fusion.96
  17.4 1.6 %fusion.38 = f32[1024,384]{1,0:T(8,128)S(1)} fusion(bf16[1024,384]{1,0:T(8,128)(2,1)S(1)} %bitcast.165, bf16[3,3,3,384,384]{4,3,2,1,0:T(8,128)(2,1)} %param.8), kind=kOutput, calls=%fused_computation.47 | convolution fusion | flops 301989888 | bytes 2654208 | tf_op jit(solution)/shard_map/dot_general | solution.py:40
  19.0 0.6 fusion.56
  19.6 0.0 collective-permute-done.2
  19.6 0.0 collective-permute-done.3
  19.6 0.2 maximum_bitcast_fusion
  19.8 0.3 fusion.98
  20.1 1.8 %fusion.14 = f32[1024,384]{1,0:T(8,128)} fusion(bf16[1024,384]{1,0:T(8,128)(2,1)S(1)} %bitcast.159, bf16[3,3,3,384,384]{4,3,2,1,0:T(8,128)(2,1)S(1)} %copy-done.1), kind=kOutput, calls=%fused_computation.23 | convolution fusion | flops 301989888 | bytes 2654208 | tf_op jit(solution)/shard_map/dot_general | solution.py:40
  21.9 1.8 %fusion.26 = f32[1024,384]{1,0:T(8,128)} fusion(bf16[1024,384]{1,0:T(8,128)(2,1)S(1)} %bitcast.158, bf16[3,3,3,384,384]{4,3,2,1,0:T(8,128)(2,1)S(1)} %copy-done.1), kind=kOutput, calls=%fused_computation.35 | convolution fusion | flops 301989888 | bytes 2654208 | tf_op jit(solution)/shard_map/dot_general | solution.py:40
  23.7 1.8 %fusion.20 = f32[1024,384]{1,0:T(8,128)} fusion(bf16[1024,384]{1,0:T(8,128)(2,1)S(1)} %bitcast.157, bf16[3,3,3,384,384]{4,3,2,1,0:T(8,128)(2,1)S(1)} %copy-done.1), kind=kOutput, calls=%fused_computation.29 | convolution fusion | flops 301989888 | bytes 2654208 | tf_op jit(solution)/shard_map/dot_general | solution.py:40
  25.5 0.5 constant_dynamic-update-slice_fusion
  26.0 0.2 fusion.94
  26.1 1.8 %fusion.44 = f32[1024,384]{1,0:T(8,128)} fusion(bf16[1024,384]{1,0:T(8,128)(2,1)S(1)} %bitcast.163, bf16[3,3,3,384,384]{4,3,2,1,0:T(8,128)(2,1)S(1)} %copy-done.1), kind=kOutput, calls=%fused_computation.53 | convolution fusion | flops 301989888 | bytes 2654208 | tf_op jit(solution)/shard_map/dot_general | solution.py:40
  28.0 1.9 %fusion.62 = f32[1024,384]{1,0:T(8,128)} fusion(bf16[1024,384]{1,0:T(8,128)(2,1)S(1)} %bitcast.160, bf16[3,3,3,384,384]{4,3,2,1,0:T(8,128)(2,1)S(1)} %copy-done.1), kind=kOutput, calls=%fused_computation.71 | convolution fusion | flops 301989888 | bytes 2654208 | tf_op jit(solution)/shard_map/dot_general | solution.py:40
  29.8 0.1 constant_dynamic-update-slice_fusion.2
  29.9 0.2 fusion.95
  30.1 1.8 %fusion.32 = f32[1024,384]{1,0:T(8,128)} fusion(bf16[1024,384]{1,0:T(8,128)(2,1)S(1)} %bitcast.164, bf16[3,3,3,384,384]{4,3,2,1,0:T(8,128)(2,1)S(1)} %copy-done.1), kind=kOutput, calls=%fused_computation.41 | convolution fusion | flops 301989888 | bytes 2654208 | tf_op jit(solution)/shard_map/dot_general | solution.py:40
  31.8 1.8 %fusion.50 = f32[1024,384]{1,0:T(8,128)} fusion(bf16[1024,384]{1,0:T(8,128)(2,1)S(1)} %bitcast.161, bf16[3,3,3,384,384]{4,3,2,1,0:T(8,128)(2,1)S(1)} %copy-done.1), kind=kOutput, calls=%fused_computation.59 | convolution fusion | flops 301989888 | bytes 2654208 | tf_op jit(solution)/shard_map/dot_general | solution.py:40
  33.6 2.3 %select_maximum_fusion = bf16[3,6,258,384]{3,2,1,0:T(8,128)(2,1)S(1)} fusion(bf16[1,6,256,384]{3,2,1,0:T(8,128)(2,1)S(1)} %maximum_bitcast_fusion, bf16[2,1,256,384]{3,2,1,0:T(8,128)(2,1)S(1)} %collective-permute-done.1, bf16[2,4,256,384]{3,2,1,0:T(8,128)(2,1)S(1)} %copy-done, bf16[2,1,256,384]{3,2,1,0:T(8,128)(2,1)S(1)} %collective-permute-done), kind=kLoop, calls=%fused_computation.3 | loop fusion | flops 26749440 | bytes 7105536 | tf_op jit(solution)/shard_map/concatenate | solution.py:52
  35.9 5.0 %fusion.93 = (bf16[1,4,256,384]{3,2,1,0:T(8,128)(2,1)}, bf16[1,4,256,384]{3,2,1,0:T(8,128)(2,1)}, bf16[1,4,256,384]{3,2,1,0:T(8,128)(2,1)S(1)}, bf16[1,4,256,384...) fusion(bf16[3,6,258,384]{3,2,1,0:T(8,128)(2,1)S(1)} %select_max, ...), kind=kLoop, calls=%fused_computation.107 | loop fusion | bytes 28311552 | tf_op jit(solution)/shard_map/slice | solution.py:37
  40.9 2.9 %fusion.16 = f32[1024,384]{1,0:T(8,128)} fusion(bf16[1024,384]{1,0:T(8,128)(2,1)} %bitcast.155, bf16[3,3,3,384,384]{4,3,2,1,0:T(8,128)(2,1)S(1)} %copy-done.1), kind=kOutput, calls=%fused_computation.25 | convolution fusion | flops 301989888 | bytes 2654208 | tf_op jit(solution)/shard_map/dot_general | solution.py:40
  43.8 1.8 %fusion.18 = f32[1024,384]{1,0:T(8,128)} fusion(bf16[1024,384]{1,0:T(8,128)(2,1)S(1)} %bitcast.154, bf16[3,3,3,384,384]{4,3,2,1,0:T(8,128)(2,1)S(1)} %copy-done.1), kind=kOutput, calls=%fused_computation.27 | convolution fusion | flops 301989888 | bytes 2654208 | tf_op jit(solution)/shard_map/dot_general | solution.py:40
  45.6 1.8 %fusion.22 = f32[1024,384]{1,0:T(8,128)} fusion(bf16[1024,384]{1,0:T(8,128)(2,1)S(1)} %bitcast.153, bf16[3,3,3,384,384]{4,3,2,1,0:T(8,128)(2,1)S(1)} %copy-done.1), kind=kOutput, calls=%fused_computation.31 | convolution fusion | flops 301989888 | bytes 2654208 | tf_op jit(solution)/shard_map/dot_general | solution.py:40
  47.4 1.8 %fusion.24 = f32[1024,384]{1,0:T(8,128)} fusion(bf16[1024,384]{1,0:T(8,128)(2,1)S(1)} %bitcast.152, bf16[3,3,3,384,384]{4,3,2,1,0:T(8,128)(2,1)S(1)} %copy-done.1), kind=kOutput, calls=%fused_computation.33 | convolution fusion | flops 301989888 | bytes 2654208 | tf_op jit(solution)/shard_map/dot_general | solution.py:40
  49.2 1.8 %fusion.28 = f32[1024,384]{1,0:T(8,128)} fusion(bf16[1024,384]{1,0:T(8,128)(2,1)S(1)} %bitcast.151, bf16[3,3,3,384,384]{4,3,2,1,0:T(8,128)(2,1)S(1)} %copy-done.1), kind=kOutput, calls=%fused_computation.37 | convolution fusion | flops 301989888 | bytes 2654208 | tf_op jit(solution)/shard_map/dot_general | solution.py:40
  51.0 1.8 %fusion.30 = f32[1024,384]{1,0:T(8,128)} fusion(bf16[1024,384]{1,0:T(8,128)(2,1)S(1)} %bitcast.150, bf16[3,3,3,384,384]{4,3,2,1,0:T(8,128)(2,1)S(1)} %copy-done.1), kind=kOutput, calls=%fused_computation.39 | convolution fusion | flops 301989888 | bytes 2654208 | tf_op jit(solution)/shard_map/dot_general | solution.py:40
  52.8 1.8 %fusion.34 = f32[1024,384]{1,0:T(8,128)} fusion(bf16[1024,384]{1,0:T(8,128)(2,1)S(1)} %bitcast.149, bf16[3,3,3,384,384]{4,3,2,1,0:T(8,128)(2,1)S(1)} %copy-done.1), kind=kOutput, calls=%fused_computation.43 | convolution fusion | flops 301989888 | bytes 2654208 | tf_op jit(solution)/shard_map/dot_general | solution.py:40
  54.6 1.8 %fusion.36 = f32[1024,384]{1,0:T(8,128)} fusion(bf16[1024,384]{1,0:T(8,128)(2,1)S(1)} %bitcast.148, bf16[3,3,3,384,384]{4,3,2,1,0:T(8,128)(2,1)S(1)} %copy-done.1), kind=kOutput, calls=%fused_computation.45 | convolution fusion | flops 301989888 | bytes 2654208 | tf_op jit(solution)/shard_map/dot_general | solution.py:40
  56.4 1.8 %fusion.40 = f32[1024,384]{1,0:T(8,128)} fusion(bf16[1024,384]{1,0:T(8,128)(2,1)S(1)} %bitcast.147, bf16[3,3,3,384,384]{4,3,2,1,0:T(8,128)(2,1)S(1)} %copy-done.1), kind=kOutput, calls=%fused_computation.49 | convolution fusion | flops 301989888 | bytes 2654208 | tf_op jit(solution)/shard_map/dot_general | solution.py:40
  58.2 1.8 %fusion.42 = f32[1024,384]{1,0:T(8,128)} fusion(bf16[1024,384]{1,0:T(8,128)(2,1)S(1)} %bitcast.146, bf16[3,3,3,384,384]{4,3,2,1,0:T(8,128)(2,1)S(1)} %copy-done.1), kind=kOutput, calls=%fused_computation.51 | convolution fusion | flops 301989888 | bytes 2654208 | tf_op jit(solution)/shard_map/dot_general | solution.py:40
  60.0 1.8 %fusion.46 = f32[1024,384]{1,0:T(8,128)} fusion(bf16[1024,384]{1,0:T(8,128)(2,1)S(1)} %bitcast.145, bf16[3,3,3,384,384]{4,3,2,1,0:T(8,128)(2,1)S(1)} %copy-done.1), kind=kOutput, calls=%fused_computation.55 | convolution fusion | flops 301989888 | bytes 2654208 | tf_op jit(solution)/shard_map/dot_general | solution.py:40
  61.8 1.9 %fusion.48 = f32[1024,384]{1,0:T(8,128)} fusion(bf16[1024,384]{1,0:T(8,128)(2,1)S(1)} %bitcast.144, bf16[3,3,3,384,384]{4,3,2,1,0:T(8,128)(2,1)S(1)} %copy-done.1), kind=kOutput, calls=%fused_computation.57 | convolution fusion | flops 301989888 | bytes 2654208 | tf_op jit(solution)/shard_map/dot_general | solution.py:40
  63.7 1.8 %fusion.52 = f32[1024,384]{1,0:T(8,128)} fusion(bf16[1024,384]{1,0:T(8,128)(2,1)S(1)} %bitcast.143, bf16[3,3,3,384,384]{4,3,2,1,0:T(8,128)(2,1)S(1)} %copy-done.1), kind=kOutput, calls=%fused_computation.61 | convolution fusion | flops 301989888 | bytes 2654208 | tf_op jit(solution)/shard_map/dot_general | solution.py:40
  65.5 1.8 %fusion.54 = f32[1024,384]{1,0:T(8,128)} fusion(bf16[1024,384]{1,0:T(8,128)(2,1)S(1)} %bitcast.142, bf16[3,3,3,384,384]{4,3,2,1,0:T(8,128)(2,1)S(1)} %copy-done.1), kind=kOutput, calls=%fused_computation.63 | convolution fusion | flops 301989888 | bytes 2654208 | tf_op jit(solution)/shard_map/dot_general | solution.py:40
  67.3 1.8 %fusion.58 = f32[1024,384]{1,0:T(8,128)} fusion(bf16[1024,384]{1,0:T(8,128)(2,1)S(1)} %bitcast.141, bf16[3,3,3,384,384]{4,3,2,1,0:T(8,128)(2,1)S(1)} %copy-done.1), kind=kOutput, calls=%fused_computation.67 | convolution fusion | flops 301989888 | bytes 2654208 | tf_op jit(solution)/shard_map/dot_general | solution.py:40
  69.1 1.8 %fusion.60 = f32[1024,384]{1,0:T(8,128)} fusion(bf16[1024,384]{1,0:T(8,128)(2,1)S(1)} %bitcast.140, bf16[3,3,3,384,384]{4,3,2,1,0:T(8,128)(2,1)S(1)} %copy-done.1), kind=kOutput, calls=%fused_computation.69 | convolution fusion | flops 301989888 | bytes 2654208 | tf_op jit(solution)/shard_map/dot_general | solution.py:40
  70.9 1.8 %fusion.64 = f32[1024,384]{1,0:T(8,128)} fusion(bf16[1024,384]{1,0:T(8,128)(2,1)S(1)} %bitcast.139, bf16[3,3,3,384,384]{4,3,2,1,0:T(8,128)(2,1)S(1)} %copy-done.1), kind=kOutput, calls=%fused_computation.73 | convolution fusion | flops 301989888 | bytes 2654208 | tf_op jit(solution)/shard_map/dot_general | solution.py:40
  72.7 14.1 %add_add_fusion = f32[1024,384]{1,0:T(8,128)} fusion(f32[1024,384]{1,0:T(8,128)} %fusion.14, f32[1024,384]{1,0:T(8,128)} %fusion.16, f32[1024,384]{1,0:T(8,128)} %fusion.18, f32[1024,384]{1,0:T(8,128)} %fusion.20, f32[1024,384]{1,0:T(8,128)} %fusion.22, f32[1024,384]{1,0:T(8,128)} %fusion.24, f32[1024,384]{1,0:T(8,128)} %fusion.26, ...), kind=kOutput, calls=%fused_computation.20 | convolution fusion | flops 312213504 | bytes 43548672 | tf_op jit(solution)/shard_map/dot_general | solution.py:40
  86.8 2.5 %fusion.12 = bf16[4,256,384]{2,1,0:T(8,128)(2,1)} fusion(bf16[4,256,384]{2,1,0:T(8,128)(2,1)S(1)} %copy-done.2, f32[4,256,384]{2,1,0:T(8,128)} %bitcast.138, f32[384]{0:T(512)S(1)} %copy-done.5), kind=kLoop, calls=%fused_computation.19 | loop fusion | flops 1572864 | bytes 3147264 | tf_op jit(solution)/shard_map/convert_element_type | solution.py:55
  (15 shorter events, 0.1 us)
Async XLA Ops:
  0.6 10.0 %copy-start = (bf16[2,4,256,384]{3,2,1,0:T(8,128)(2,1)S(1)}, bf16[2,4,256,384]{3,2,1,0:T(8,128)(2,1)}, u32[]{:S(2)}) copy-start(bf16[2,4,256,384]{3,2,1,0:T(8,128)(2,1)} %param.6) | copy-start | bytes 4718596
  3.8 15.8 %copy-start.3 = (bf16[4,256,384]{2,1,0:T(8,128)(2,1)}, bf16[4,256,384]{2,1,0:T(8,128)(2,1)S(1)}, u32[]{:S(2)}) copy-start(bf16[4,256,384]{2,1,0:T(8,128)(2,1)S(1)} %fusion.11) | copy-start | bytes 2359300
  3.8 15.1 %copy-start.1 = (bf16[3,3,3,384,384]{4,3,2,1,0:T(8,128)(2,1)S(1)}, bf16[3,3,3,384,384]{4,3,2,1,0:T(8,128)(2,1)}, u32[]{:S(2)}) copy-start(bf16[3,3,3,384,384]{4,3,2,1,0:T(8,128)(2,1)} %param.8) | copy-start | bytes 23887876
  3.9 15.7 %collective-permute-start.2 = (bf16[1,256,384]{2,1,0:T(8,128)(2,1)S(1)}, bf16[1,256,384]{2,1,0:T(8,128)(2,1)S(1)}, u32[]{:S(2)}, u32[]{:S(2)}) collective-permute-start(bf16[1,256,384]{2,1,0:T(8,128)(2,1)S(1)} %get-tuple-element.33), channel_id=1, source_target_pairs={{0,1},{1,2},{2,3},{3,4},{4,5},{5,6},{6,7},{7,8},{8,9},{9,10},{10,1... | collective-permute-start | bytes 589832 | tf_op jit(solution)/shard_map/ppermute | solution.py:14
  6.2 13.4 %collective-permute-start.3 = (bf16[1,256,384]{2,1,0:T(8,128)(2,1)S(1)}, bf16[1,256,384]{2,1,0:T(8,128)(2,1)S(1)}, u32[]{:S(2)}, u32[]{:S(2)}) collective-permute-start(bf16[1,256,384]{2,1,0:T(8,128)(2,1)S(1)} %get-tuple-element.34), channel_id=1, source_target_pairs={{1,0},{2,1},{3,2},{4,3},{5,4},{6,5},{7,6},{8,7},{9,8},{10,9},{11,1... | collective-permute-start | bytes 589832 | tf_op jit(solution)/shard_map/ppermute | solution.py:17
  10.7 14.7 %collective-permute-start = (bf16[2,1,256,384]{3,2,1,0:T(8,128)(2,1)S(1)}, bf16[2,1,256,384]{3,2,1,0:T(8,128)(2,1)S(1)}, u32[]{:S(2)}, u32[]{:S(2)}) collective-permute-start(bf16[2,1,256,384]{3,2,1,0:T(8,128)(2,1)S(1)} %get-tuple-element.28), channel_id=1, source_target_pairs={{0,1},{1,2},{2,3},{3,4},{4,5},{5,6},{6,7},{7,8},{8,9},{9,10},{10,1... | collective-permute-start | bytes 1179656 | tf_op jit(solution)/shard_map/ppermute | solution.py:14
  12.6 17.2 %collective-permute-start.1 = (bf16[2,1,256,384]{3,2,1,0:T(8,128)(2,1)S(1)}, bf16[2,1,256,384]{3,2,1,0:T(8,128)(2,1)S(1)}, u32[]{:S(2)}, u32[]{:S(2)}) collective-permute-start(bf16[2,1,256,384]{3,2,1,0:T(8,128)(2,1)S(1)} %get-tuple-element.29), channel_id=1, source_target_pairs={{1,0},{2,1},{3,2},{4,3},{5,4},{6,5},{7,6},{8,7},{9,8},{10,9},{11,1... | collective-permute-start | bytes 1179656 | tf_op jit(solution)/shard_map/ppermute | solution.py:17
  70.9 1.8 %copy-start.4 = (bf16[1,4,256,384]{3,2,1,0:T(8,128)(2,1)S(1)}, bf16[1,4,256,384]{3,2,1,0:T(8,128)(2,1)}, u32[]{:S(2)}) copy-start(bf16[1,4,256,384]{3,2,1,0:T(8,128)(2,1)} %get-tuple-element.2) | copy-start | bytes 2359300
  72.7 14.1 %copy-start.2 = (bf16[4,256,384]{2,1,0:T(8,128)(2,1)S(1)}, bf16[4,256,384]{2,1,0:T(8,128)(2,1)}, u32[]{:S(2)}) copy-start(bf16[4,256,384]{2,1,0:T(8,128)(2,1)} %param.5) | copy-start | bytes 2359300
  72.7 14.1 %copy-start.5 = (f32[384]{0:T(512)S(1)}, f32[384]{0:T(512)}, u32[]{:S(2)}) copy-start(f32[384]{0:T(512)} %param.9) | copy-start | bytes 4612
where the time goes:
time: 89.6 us; the launch traced here: 89.3 us
  matrix products  60.7 us (68%)
  starting transfers between devices  13.2 us (15%)
  other arithmetic  8.09 us (9%)
  local copies, waits for them, and re-layouts  6.45 us (7%)
    dot_general x27, matrix products, tap_products(): jnp.dot(window.reshape(out_rows * out_cols, channels), weight[tap_time, t...  60.7 us
    ppermute x2, starting transfers between devices, extended(): lax.ppermute(lax.slice_in_dim(block, 0, width, axis=dim), axis, backward)  8.95 us
    slice x5, local copies, waits for them, and re-layouts, tap_products(): frames[tap_time, tap_row:tap_row + out_rows, tap_col:tap_col + out_cols, :]  5.74 us
    ppermute x2, starting transfers between devices, extended(): lax.ppermute(lax.slice_in_dim(block, block.shape[dim] - width, None, axis...  4.24 us
    convert_element_type x1, other arithmetic, on_device(): decoded = (latent.astype(jnp.float32) + branch).astype(jnp.bfloat16)  2.48 us
    concatenate x1, other arithmetic, on_device(): frames = jnp.concatenate([cache_ext, frame_ext[None]], axis=0)  2.28 us
  transfers between devices with their start and end apart: 4, of which 0 were waited for; matrix products, arithmetic and copies ran while one was open for 14% of the time, Pallas kernels for 0%

commit v1 on v0

v1 whole, which is shorter than its diff:
```python
import functools

import jax
import jax.numpy as jnp
from jax import lax
from jax.experimental import pallas as pl
from jax.experimental.pallas import tpu as pltpu
from jax.sharding import PartitionSpec as P

epsilon = 1e-06
MESH = pl.DeviceIdType.MESH
f32 = jnp.float32
bf16 = jnp.bfloat16


def act(values, gain):
    values = values.astype(f32)
    scaled = values * lax.rsqrt(jnp.mean(values * values, axis=-1, keepdims=True) + epsilon) * gain
    return (scaled * jax.nn.sigmoid(scaled)).astype(bf16)


def kernel(
    shape, latent, cache, gain, weight, bias, decoded, next_cache,
    xs, ws, lat, acc, out, sent, got, x_sem, w_sem, o_sem, n_sem, send_sem, recv_sem,
):
    count, rows, cols, chan = shape
    last = rows - 1
    me = lax.axis_index("rows")
    has_up, has_down = me > 0, me < count - 1
    wide = 3 * chan

    def span(row):
        return pl.ds(row * cols, cols)

    def centre(time):
        return pl.ds(time * wide + chan, chan)

    x_in = {}
    for time in range(3):
        for row in range(rows):
            if time < 2:
                src, dst = cache.at[time, row], xs.at[span(row), centre(time)]
            else:
                src, dst = latent.at[row], lat.at[span(row)]
            x_in[time, row] = pltpu.make_async_copy(src, dst, x_sem.at[time, row])
    w_in = {}
    for time in range(3):
        for tap in range(3):
            for col in range(3):
                w_in[time, tap, col] = pltpu.make_async_copy(
                    weight.at[time, tap, col],
                    ws.at[pl.ds(time * wide + col * chan, chan), pl.ds(tap * chan, chan)],
                    w_sem.at[time, tap, col],
                )
    middle = list(range(1, last))
    for time in (0, 2, 1):
        for row in (0, last):
            x_in[time, row].start()
        if time == 0:
            for tap in (2, 0):
                for col in range(3):
                    w_in[time, tap, col].start()
    for time in (1, 2):
        for tap in (2, 0):
            for col in range(3):
                w_in[time, tap, col].start()
    for time in range(3):
        for row in middle:
            x_in[time, row].start()
    for time in range(3):
        for col in range(3):
            w_in[time, 1, col].start()

    barrier = pltpu.get_barrier_semaphore()

    @pl.when(has_up)
    def _():
        pl.semaphore_signal(barrier, inc=1, device_id={"rows": me - 1}, device_id_type=MESH)

    @pl.when(has_down)
    def _():
        pl.semaphore_signal(barrier, inc=1, device_id={"rows": me + 1}, device_id_type=MESH)

    place = lax.broadcasted_iota(jnp.int32, (cols, chan), 0)

    def shifts(time, row, value):
        value = value.astype(f32)
        before = jnp.where(place == 0, 0.0, pltpu.roll(value, 1, 0)).astype(bf16)
        after = jnp.where(place == cols - 1, 0.0, pltpu.roll(value, cols - 1, 0)).astype(bf16)
        xs[span(row), pl.ds(time * wide, chan)] = before
        xs[span(row), pl.ds(time * wide + 2 * chan, chan)] = after

    n_out = []

    def prepare(time, row):
        x_in[time, row].wait()
        if time < 2:
            shifts(time, row, xs[span(row), centre(time)])
        else:
            value = act(lat[span(row)], gain[...])
            xs[span(row), centre(time)] = value
            copy = pltpu.make_async_copy(
                xs.at[span(row), centre(time)], next_cache.at[row], n_sem.at[row]
            )
            copy.start()
            n_out.append(copy)
            shifts(time, row, value)

    def dot(row, times, taps):
        depth = pl.ds(times[0] * wide, len(times) * wide)
        width = pl.ds(taps[0] * chan, len(taps) * chan)
        return jnp.dot(xs[span(row), depth], ws[depth, width], preferred_element_type=f32)

    edges = ((0, 2), (last, 0))
    for time in range(3):
        for row, _ in edges:
            prepare(time, row)
        for row, tap in edges:
            for col in range(3):
                w_in[time, tap, col].wait()
    for side, (row, tap) in enumerate(edges):
        sent[side] = dot(row, (0, 1, 2), (tap,)).astype(bf16)

    pl.semaphore_wait(barrier, has_up.astype(jnp.int32) + has_down.astype(jnp.int32))

    def remote(side, target):
        return pltpu.make_async_remote_copy(
            src_ref=sent.at[side],
            dst_ref=got.at[side],
            send_sem=send_sem.at[side],
            recv_sem=recv_sem.at[side],
            device_id={"rows": target},
            device_id_type=MESH,
        )

    upward, downward = remote(0, me - 1), remote(1, me + 1)
    pl.when(has_up)(upward.start)
    pl.when(has_down)(downward.start)

    for row in middle:
        for time in range(3):
            prepare(time, row)
    for time in range(3):
        for col in range(3):
            w_in[time, 1, col].wait()

    started = set()

    def add(target, value):
        if target in started:
            acc[span(target)] += value
        else:
            started.add(target)
            acc[span(target)] = lat[span(target)].astype(f32) + bias[...] + value

    o_out = []

    def finish(target):
        out[span(target)] = acc[span(target)].astype(bf16)
        copy = pltpu.make_async_copy(out.at[span(target)], decoded.at[target], o_sem.at[target])
        copy.start()
        o_out.append(copy)

    left = {target: sum(0 <= target + tap - 1 < rows for tap in range(3)) for target in range(rows)}
    for row in middle + [0, last]:
        taps = [tap for tap in range(3) if 0 <= row - tap + 1 < rows]
        value = dot(row, (0, 1, 2), taps)
        for at, tap in enumerate(taps):
            target = row - tap + 1
            add(target, value[:, at * chan : (at + 1) * chan])
            left[target] -= 1
            if left[target] == 0 and 0 < target < last:
                finish(target)

    @pl.when(has_up)
    def _():
        upward.wait_send()
        downward.wait_recv()
        acc[span(0)] += got[1].astype(f32)

    finish(0)

    @pl.when(has_down)
    def _():
        downward.wait_send()
        upward.wait_recv()
        acc[span(last)] += got[0].astype(f32)

    finish(last)
    for copy in n_out + o_out:
        copy.wait()


def on_device(latent, cache_frames, norm_gain, weight, bias):
    rows, cols, chan = latent.shape
    count = lax.axis_size("rows")
    anywhere = pl.BlockSpec(memory_space=pl.ANY)
    vmem = pl.BlockSpec(memory_space=pltpu.VMEM)
    size = rows * cols
    DMA = pltpu.SemaphoreType.DMA
    return pl.pallas_call(
        functools.partial(kernel, (count, rows, cols, chan)),
        out_shape=[jax.ShapeDtypeStruct(latent.shape, bf16)] * 2,
        in_specs=[anywhere, anywhere, vmem, anywhere, vmem],
        out_specs=[anywhere, anywhere],
        scratch_shapes=[
            pltpu.VMEM((size, 9 * chan), bf16),
            pltpu.VMEM((9 * chan, 3 * chan), bf16),
            pltpu.VMEM((size, chan), bf16),
            pltpu.VMEM((size, chan), f32),
            pltpu.VMEM((size, chan), bf16),
            pltpu.VMEM((2, cols, chan), bf16),
            pltpu.VMEM((2, cols, chan), bf16),
            DMA((3, rows)),
            DMA((3, 3, 3)),
            DMA((rows,)),
            DMA((rows,)),
            DMA((2,)),
            DMA((2,)),
        ],
        compiler_params=pltpu.CompilerParams(
            collective_id=0, has_side_effects=True, vmem_limit_bytes=56 * 2**20
        ),
        cost_estimate=pl.CostEstimate(
            flops=2 * size * 27 * chan * chan,
            bytes_accessed=2 * (5 * size * chan + 27 * chan * chan),
            transcendentals=size * chan,
        ),
    )(latent, cache_frames, norm_gain.reshape(1, chan), weight, bias.reshape(1, chan))


def solution(mesh):
    in_specs = (
        P(("groups", "rows"), None, None),
        P(None, ("groups", "rows"), None, None),
        P(),
        P(),
        P(),
    )
    out_specs = (P(("groups", "rows"), None, None), P(("groups", "rows"), None, None))
    return jax.shard_map(
        on_device, mesh=mesh, in_specs=in_specs, out_specs=out_specs, check_vma=False
    )
```

time: 89.6 us -> 24 us (0.27)
  matrix products: 60.7 us -> 0 us
  Pallas kernels: 0 us -> 16.4 us
  starting transfers between devices: 13.2 us -> 0 us
  other arithmetic: 8.09 us -> 0 us
    dot_general x27 -> x0, matrix products: 60.7 us -> none  [tap_products(): jnp.dot(window.reshape(out_rows * out_cols, channels), weight[tap_time, t...]
    pallas_call x0 -> x1, Pallas kernels: none -> 16.4 us  [on_device(): pl.pallas_call(functools.partial(kernel, (count, rows, cols, chan)), out_...]
    ppermute x4 -> x0, starting transfers between devices: 13.2 us -> none  [the longest x2 8.95 us: extended(): lax.ppermute(lax.slice_in_dim(block, 0, width, axis=dim), axis, backward)]
    slice x7 -> x0, local copies, waits for them, and re-layouts: 5.86 us -> none  [the longest x5 5.74 us: tap_products(): frames[tap_time, tap_row:tap_row + out_rows, tap_col:tap_col + out_cols, :]]
    convert_element_type x2 -> x0, other arithmetic: 4.15 us -> none  [the longest x1 2.48 us: on_device(): decoded = (latent.astype(jnp.float32) + branch).astype(jnp.bfloat16)]
    unnamed x13 -> x2, local copies, waits for them, and re-layouts: 0.07 us -> 4.18 us
    reshape x0 -> x2, local copies, waits for them, and re-layouts: none -> 2.49 us  [the longest x1 1.25 us: on_device(): norm_gain.reshape(1, chan)]
    concatenate x1 -> x0, other arithmetic: 2.28 us -> none  [on_device(): frames = jnp.concatenate([cache_ext, frame_ext[None]], axis=0)]
  transfers between devices with their start and end apart: 4 -> 0, of which waited for: 0 -> 0; matrix products, arithmetic and copies ran while one was open for 14% -> 0% of each run, Pallas kernels for 0% -> 0%
where the time goes in v1:
time: 24 us; the launch traced here: 23.7 us
  Pallas kernels  16.4 us (68%)
  local copies, waits for them, and re-layouts  6.67 us (28%)
  between operations  0.64 us (3%)
    pallas_call x1, Pallas kernels, on_device(): pl.pallas_call(functools.partial(kernel, (count, rows, cols, chan)), out_...  16.4 us
    unnamed x2, local copies, waits for them, and re-layouts  4.18 us
    reshape x1, local copies, waits for them, and re-layouts, on_device(): norm_gain.reshape(1, chan)  1.25 us
    reshape x1, local copies, waits for them, and re-layouts, on_device(): bias.reshape(1, chan)  1.24 us

profile of v1, /device:TPU:24, one launch (start us, length us, event | category | flops | bytes accessed | tf_op | source)
XLA Modules:
  0.0 23.7 jit_solution(10841682609879189749)
XLA Ops:
  0.6 1.2 %reshape.10.gain = f32[1,384]{1,0:T(1,128)} reshape(f32[384]{0:T(512)} %param.7) | data formatting | bytes 3072 | tf_op jit(solution)/shard_map/reshape | solution.py:229
  1.9 1.2 %reshape.11.bias = f32[1,384]{1,0:T(1,128)} reshape(f32[384]{0:T(512)} %param.9) | data formatting | bytes 3072 | tf_op jit(solution)/shard_map/reshape | solution.py:229
  3.1 16.4 %shard_map.68 = (bf16[4,256,384]{2,1,0:T(8,128)(2,1)}, bf16[4,256,384]{2,1,0:T(8,128)(2,1)}) custom-call(bf16[4,256,384]{2,1,0:T(8,128)(2,1)} %latent.1, bf16[2,4,256,384]{3,2,1,0:T(8,128)(2,1)} %cache.1, f32[1,384]{1,0:T(1,128)} %reshape.10.gain, bf16[3,3,3,384,384]{4,3,2,1,0:T(8,128)(2,1)} %weight.1, f32[1,384]{1,0:T(1,128)} %reshape.11.bias), custom_call_target="tpu_custom_call" | custom-call | flops 8153726976 | bytes 11894784 | tf_op jit(solution)/shard_map/pallas_call | solution.py:201
  19.5 2.1 %copy.9 = bf16[4,256,384]{2,1,0:T(8,128)(2,1)} copy(bf16[4,256,384]{2,1,0:T(8,128)(2,1)} %get-tuple-element.4) | data formatting | bytes 1572864
  21.6 2.1 %copy.10 = bf16[4,256,384]{2,1,0:T(8,128)(2,1)} copy(bf16[4,256,384]{2,1,0:T(8,128)(2,1)} %get-tuple-element.5) | data formatting | bytes 1572864

commit v2 on v1

v2 whole, which is shorter than its diff:
```python
import functools

import jax
import jax.numpy as jnp
from jax import lax
from jax.experimental import pallas as pl
from jax.experimental.pallas import tpu as pltpu
from jax.sharding import PartitionSpec as P

epsilon = 1e-06
MESH = pl.DeviceIdType.MESH
f32 = jnp.float32
bf16 = jnp.bfloat16


def act(values, gain):
    values = values.astype(f32)
    scaled = values * lax.rsqrt(jnp.mean(values * values, axis=-1, keepdims=True) + epsilon) * gain
    return (scaled * jax.nn.sigmoid(scaled)).astype(bf16)


def kernel(
    shape, latent, cache, gain_in, weight, bias_in, acc, fresh, got,
    xs, ws, lat, part, sent, gain, bias, p_sem, x_sem, w_sem, send_sem, recv_sem,
):
    count, rows, cols, chan = shape
    last = rows - 1
    me = lax.axis_index("rows")
    has_up, has_down = me > 0, me < count - 1
    wide = 3 * chan

    def span(row, many=1):
        return pl.ds(row * cols, many * cols)

    def centre(time):
        return pl.ds(time * wide + chan, chan)

    x_in = {}
    for time in range(3):
        for row in range(rows):
            if time < 2:
                src, dst = cache.at[time, row], xs.at[span(row), centre(time)]
            else:
                src, dst = latent.at[row], lat.at[span(row)]
            x_in[time, row] = pltpu.make_async_copy(src, dst, x_sem.at[time, row])
    w_in = {}
    for time in range(3):
        for tap in range(3):
            for col in range(3):
                w_in[time, tap, col] = pltpu.make_async_copy(
                    weight.at[time, tap, col],
                    ws.at[pl.ds(time * wide + col * chan, chan), pl.ds(tap * chan, chan)],
                    w_sem.at[time, tap, col],
                )

    def weights(time, taps, act):
        for tap in taps:
            for col in range(3):
                getattr(w_in[time, tap, col], act)()

    vectors = [
        pltpu.make_async_copy(src, dst, p_sem.at[at])
        for at, (src, dst) in enumerate(((gain_in, gain), (bias_in, bias)))
    ]
    middle = list(range(1, last))
    for copy in vectors:
        copy.start()
    for time in (2, 0, 1):
        for row in (0, last):
            x_in[time, row].start()
    weights(0, (2, 0), "start")
    for row in middle:
        for time in range(3):
            x_in[time, row].start()
    weights(1, (2, 0), "start")
    weights(2, (2, 0), "start")
    for time in range(3):
        weights(time, (1,), "start")

    barrier = pltpu.get_barrier_semaphore()

    @pl.when(has_up)
    def _():
        pl.semaphore_signal(barrier, inc=1, device_id={"rows": me - 1}, device_id_type=MESH)

    @pl.when(has_down)
    def _():
        pl.semaphore_signal(barrier, inc=1, device_id={"rows": me + 1}, device_id_type=MESH)

    place = lax.broadcasted_iota(jnp.int32, (cols, chan), 0)

    def shifts(time, row, value):
        value = value.astype(f32)
        before = jnp.where(place == 0, 0.0, pltpu.roll(value, 1, 0)).astype(bf16)
        after = jnp.where(place == cols - 1, 0.0, pltpu.roll(value, cols - 1, 0)).astype(bf16)
        xs[span(row), pl.ds(time * wide, chan)] = before
        xs[span(row), pl.ds(time * wide + 2 * chan, chan)] = after

    def prepare(row):
        value = act(lat[span(row)], gain[...].reshape(1, chan))
        xs[span(row), centre(2)] = value
        fresh[row] = value
        shifts(2, row, value)
        for time in range(2):
            shifts(time, row, xs[span(row), centre(time)])

    def dot(rows_of, times, taps):
        depth = pl.ds(times[0] * wide, len(times) * wide)
        width = pl.ds(taps[0] * chan, len(taps) * chan)
        return jnp.dot(xs[rows_of, depth], ws[depth, width], preferred_element_type=f32)

    edges = ((0, 2), (last, 0))
    for copy in vectors:
        copy.wait()
    for row, _ in edges:
        for time in range(3):
            x_in[time, row].wait()
        prepare(row)
    for row in middle:
        for time in range(3):
            x_in[time, row].wait()
    todo = list(middle)
    for time in range(3):
        weights(time, (2, 0), "wait")
        for side, (row, tap) in enumerate(edges):
            value = dot(span(row), (time,), (tap,))
            if time == 0:
                part[side] = value
            elif time == 1:
                part[side] += value
            else:
                sent[side] = (part[side] + value).astype(bf16)
        if time < 2:
            share = -(-len(middle) // 2)
            for row in todo[:share]:
                prepare(row)
            todo = todo[share:]

    pl.semaphore_wait(barrier, has_up.astype(jnp.int32) + has_down.astype(jnp.int32))

    def remote(side, target):
        return pltpu.make_async_remote_copy(
            src_ref=sent.at[side],
            dst_ref=got.at[side],
            send_sem=send_sem.at[side],
            recv_sem=recv_sem.at[side],
            device_id={"rows": target},
            device_id_type=MESH,
        )

    upward, downward = remote(0, me - 1), remote(1, me + 1)
    pl.when(has_up)(upward.start)
    pl.when(has_down)(downward.start)
    for time in range(3):
        weights(time, (1,), "wait")

    started = set()

    def add(target, value):
        if target in started:
            acc[target] += value
        else:
            started.add(target)
            acc[target] = lat[span(target)].astype(f32) + bias[...].reshape(1, chan) + value

    def own(row, many, taps):
        value = dot(span(row, many), (0, 1, 2), taps)
        for step in range(many):
            for at, tap in enumerate(taps):
                add(
                    row + step - tap + 1,
                    value[step * cols : (step + 1) * cols, at * chan : (at + 1) * chan],
                )

    for row in middle[::2]:
        own(row, min(2, last - row), (0, 1, 2))
    own(0, 1, (0, 1))
    own(last, 1, (1, 2))

    @pl.when(has_up)
    def _():
        upward.wait_send()
        downward.wait_recv()

    @pl.when(has_down)
    def _():
        downward.wait_send()
        upward.wait_recv()

    @pl.when(jnp.logical_not(has_up))
    def _():
        got[1] = jnp.zeros((cols, chan), bf16)

    @pl.when(jnp.logical_not(has_down))
    def _():
        got[0] = jnp.zeros((cols, chan), bf16)


def writer(acc, fresh, got, decoded, next_cache, out, sem):
    rows = acc.shape[0]
    copies = [pltpu.make_async_copy(fresh, next_cache, sem.at[rows])]
    copies[0].start()
    for row in range(rows):
        value = acc[row]
        if row == 0:
            value = value + got[1].astype(f32)
        if row == rows - 1:
            value = value + got[0].astype(f32)
        out[row] = value.astype(bf16)
        copy = pltpu.make_async_copy(out.at[row], decoded.at[row], sem.at[row])
        copy.start()
        copies.append(copy)
    for copy in copies:
        copy.wait()


def on_device(latent, cache_frames, norm_gain, weight, bias):
    rows, cols, chan = latent.shape
    count = lax.axis_size("rows")
    arguments = (latent, cache_frames, norm_gain, weight, bias)
    hbm = pl.BlockSpec(memory_space=pltpu.HBM)
    vmem = pl.BlockSpec(memory_space=pltpu.VMEM)
    size = rows * cols
    DMA = pltpu.SemaphoreType.DMA
    acc, fresh, got = pl.pallas_call(
        functools.partial(kernel, (count, rows, cols, chan)),
        out_shape=[
            pltpu.VMEM((rows, cols, chan), f32),
            pltpu.VMEM((rows, cols, chan), bf16),
            pltpu.VMEM((2, cols, chan), bf16),
        ],
        in_specs=[hbm] * 5,
        out_specs=[vmem] * 3,
        scratch_shapes=[
            pltpu.VMEM((size, 9 * chan), bf16),
            pltpu.VMEM((9 * chan, 3 * chan), bf16),
            pltpu.VMEM((size, chan), bf16),
            pltpu.VMEM((2, cols, chan), f32),
            pltpu.VMEM((2, cols, chan), bf16),
            pltpu.VMEM((chan,), f32),
            pltpu.VMEM((chan,), f32),
            DMA((2,)),
            DMA((3, rows)),
            DMA((3, 3, 3)),
            DMA((2,)),
            DMA((2,)),
        ],
        compiler_params=pltpu.CompilerParams(
            collective_id=0, has_side_effects=True, vmem_limit_bytes=40 * 2**20
        ),
        cost_estimate=pl.CostEstimate(
            flops=2 * size * 27 * chan * chan,
            bytes_accessed=2 * (5 * size * chan + 27 * chan * chan),
            transcendentals=size * chan,
        ),
    )(*(pltpu.with_memory_space_constraint(array, pltpu.HBM) for array in arguments))
    return pl.pallas_call(
        writer,
        out_shape=[jax.ShapeDtypeStruct(latent.shape, bf16)] * 2,
        in_specs=[vmem] * 3,
        out_specs=[hbm] * 2,
        scratch_shapes=[pltpu.VMEM((rows, cols, chan), bf16), DMA((rows + 1,))],
        compiler_params=pltpu.CompilerParams(vmem_limit_bytes=16 * 2**20),
        cost_estimate=pl.CostEstimate(
            flops=size * chan, bytes_accessed=10 * size * chan, transcendentals=0
        ),
    )(acc, fresh, got)


def solution(mesh):
    in_specs = (
        P(("groups", "rows"), None, None),
        P(None, ("groups", "rows"), None, None),
        P(),
        P(),
        P(),
    )
    out_specs = (P(("groups", "rows"), None, None), P(("groups", "rows"), None, None))
    return jax.shard_map(
        on_device, mesh=mesh, in_specs=in_specs, out_specs=out_specs, check_vma=False
    )
```

time: 24 us -> 17.6 us (0.73)
  local copies, waits for them, and re-layouts: 6.67 us -> 0 us
  Pallas kernels: 16.4 us -> 16.8 us
    unnamed x2 -> x0, local copies, waits for them, and re-layouts: 4.18 us -> none
    reshape x2 -> x0, local copies, waits for them, and re-layouts: 2.49 us -> none  [the longest x1 1.25 us: on_device(): norm_gain.reshape(1, chan)]
    pallas_call x0 -> x1, Pallas kernels: none -> 1.17 us  [on_device(): pl.pallas_call(writer, out_shape=[jax.ShapeDtypeStruct(latent.shape, bf16...]
    pallas_call x1, Pallas kernels: 16.4 us -> 15.6 us  [on_device(): pl.pallas_call(functools.partial(kernel, (count, rows, cols, chan)), out_...]
where the time goes in v2:
time: 17.6 us; the launch traced here: 17.4 us
  Pallas kernels  16.8 us (95%)
  between operations  0.64 us (4%)
    pallas_call x1, Pallas kernels, on_device(): pl.pallas_call(functools.partial(kernel, (count, rows, cols, chan)), out_...  15.6 us
    pallas_call x1, Pallas kernels, on_device(): pl.pallas_call(writer, out_shape=[jax.ShapeDtypeStruct(latent.shape, bf16...  1.17 us

profile of v2, /device:TPU:24, one launch (start us, length us, event | category | flops | bytes accessed | tf_op | source)
XLA Modules:
  0.0 17.4 jit_solution(3666835167146847977)
XLA Ops:
  0.6 15.6 %shard_map.68 = (f32[4,256,384]{2,1,0:T(8,128)S(1)}, bf16[4,256,384]{2,1,0:T(8,128)(2,1)S(1)}, bf16[2,256,384]{2,1,0:T(8,128)(2,1)S(1)}) custom-call(bf16[4,256,384]{2,1,0:T(8,128)(2,1)} %latent.1, bf16[2,4,256,384]{3,2,1,0:T(8,128)(2,1)} %cache.1, f32[384]{0:T(512)} %gain_in.1, bf16[3,3,3,384,384]{4,3,2,1,0:T(8,128)(2,1)} %weight.1, f32[384]{0:T(512)} %bias_in.1), custom_call_target="tpu_custom_call" | custom-call | flops 8153726976 | bytes 11894784 | tf_op jit(solution)/shard_map/pallas_call | solution.py:225
  16.3 1.2 %shard_map.69 = (bf16[4,256,384]{2,1,0:T(8,128)(2,1)}, bf16[4,256,384]{2,1,0:T(8,128)(2,1)}) custom-call(f32[4,256,384]{2,1,0:T(8,128)S(1)} %get-tuple-element.5.acc, bf16[4,256,384]{2,1,0:T(8,128)(2,1)S(1)} %get-tuple-element.6.fresh, bf16[2,256,384]{2,1,0:T(8,128)(2,1)S(1)} %get-tuple-element.7.got), custom_call_target="tpu_custom_call" | custom-call | flops 393216 | bytes 3932160 | tf_op jit(solution)/shard_map/pallas_call | solution.py:257

commit v3 on v2

--- a/solution.py
+++ b/solution.py
@@ -65,15 +65,13 @@
     middle = list(range(1, last))
     for copy in vectors:
         copy.start()
-    for time in (2, 0, 1):
+    for time in range(3):
         for row in (0, last):
             x_in[time, row].start()
-    weights(0, (2, 0), "start")
+        weights(time, (2, 0), "start")
     for row in middle:
         for time in range(3):
             x_in[time, row].start()
-    weights(1, (2, 0), "start")
-    weights(2, (2, 0), "start")
     for time in range(3):
         weights(time, (1,), "start")
 
@@ -87,22 +85,27 @@
     def _():
         pl.semaphore_signal(barrier, inc=1, device_id={"rows": me + 1}, device_id_type=MESH)
 
-    place = lax.broadcasted_iota(jnp.int32, (cols, chan), 0)
+    place = lax.broadcasted_iota(jnp.int32, (16, chan), 0)
 
     def shifts(time, row, value):
         value = value.astype(f32)
-        before = jnp.where(place == 0, 0.0, pltpu.roll(value, 1, 0)).astype(bf16)
-        after = jnp.where(place == cols - 1, 0.0, pltpu.roll(value, cols - 1, 0)).astype(bf16)
+        before = pltpu.roll(value, 1, 0)
+        after = pltpu.roll(value, cols - 1, 0)
+        head = jnp.where(place == 0, 0.0, before[:16])
+        tail = jnp.where(place == 15, 0.0, after[cols - 16 :])
+        before = jnp.concatenate([head, before[16:]], axis=0).astype(bf16)
+        after = jnp.concatenate([after[: cols - 16], tail], axis=0).astype(bf16)
         xs[span(row), pl.ds(time * wide, chan)] = before
         xs[span(row), pl.ds(time * wide + 2 * chan, chan)] = after
 
-    def prepare(row):
+    def prepare(time, row):
+        if time < 2:
+            shifts(time, row, xs[span(row), centre(time)])
+            return
         value = act(lat[span(row)], gain[...].reshape(1, chan))
         xs[span(row), centre(2)] = value
         fresh[row] = value
         shifts(2, row, value)
-        for time in range(2):
-            shifts(time, row, xs[span(row), centre(time)])
 
     def dot(rows_of, times, taps):
         depth = pl.ds(times[0] * wide, len(times) * wide)
@@ -113,15 +116,14 @@
     for copy in vectors:
         copy.wait()
     for row, _ in edges:
-        for time in range(3):
-            x_in[time, row].wait()
-        prepare(row)
-    for row in middle:
-        for time in range(3):
-            x_in[time, row].wait()
-    todo = list(middle)
+        x_in[0, row].wait()
+    for row, _ in edges:
+        prepare(0, row)
     for time in range(3):
         weights(time, (2, 0), "wait")
+        if time < 2:
+            for row, _ in edges:
+                x_in[time + 1, row].wait()
         for side, (row, tap) in enumerate(edges):
             value = dot(span(row), (time,), (tap,))
             if time == 0:
@@ -130,11 +132,8 @@
                 part[side] += value
             else:
                 sent[side] = (part[side] + value).astype(bf16)
-        if time < 2:
-            share = -(-len(middle) // 2)
-            for row in todo[:share]:
-                prepare(row)
-            todo = todo[share:]
+            if time < 2:
+                prepare(time + 1, row)
 
     pl.semaphore_wait(barrier, has_up.astype(jnp.int32) + has_down.astype(jnp.int32))
 
@@ -151,6 +150,9 @@
     upward, downward = remote(0, me - 1), remote(1, me + 1)
     pl.when(has_up)(upward.start)
     pl.when(has_down)(downward.start)
+    for row in middle:
+        for time in range(3):
+            x_in[time, row].wait()
     for time in range(3):
         weights(time, (1,), "wait")
 
@@ -172,10 +174,13 @@
                     value[step * cols : (step + 1) * cols, at * chan : (at + 1) * chan],
                 )
 
+    own(0, 1, (0, 1))
+    for row in middle:
+        for time in range(3):
+            prepare(time, row)
+    own(last, 1, (1, 2))
     for row in middle[::2]:
         own(row, min(2, last - row), (0, 1, 2))
-    own(0, 1, (0, 1))
-    own(last, 1, (1, 2))
 
     @pl.when(has_up)
     def _():

time: 17.6 us -> 16.9 us (0.960)
  Pallas kernels: 16.8 us -> 16.1 us
    pallas_call x1, Pallas kernels: 15.6 us -> 14.9 us  [on_device(): pl.pallas_call(functools.partial(kernel, (count, rows, cols, chan)), out_...]
where the time goes in v3:
time: 16.9 us; the launch traced here: 16.7 us
  Pallas kernels  16.1 us (95%)
  between operations  0.64 us (4%)
    pallas_call x1, Pallas kernels, on_device(): pl.pallas_call(functools.partial(kernel, (count, rows, cols, chan)), out_...  14.9 us
    pallas_call x1, Pallas kernels, on_device(): pl.pallas_call(writer, out_shape=[jax.ShapeDtypeStruct(latent.shape, bf16...  1.17 us

profile of v3, /device:TPU:24, one launch (start us, length us, event | category | flops | bytes accessed | tf_op | source)
XLA Modules:
  0.0 16.7 jit_solution(8441107763161900831)
XLA Ops:
  0.6 14.9 %shard_map.68 = (f32[4,256,384]{2,1,0:T(8,128)S(1)}, bf16[4,256,384]{2,1,0:T(8,128)(2,1)S(1)}, bf16[2,256,384]{2,1,0:T(8,128)(2,1)S(1)}) custom-call(bf16[4,256,384]{2,1,0:T(8,128)(2,1)} %latent.1, bf16[2,4,256,384]{3,2,1,0:T(8,128)(2,1)} %cache.1, f32[384]{0:T(512)} %gain_in.1, bf16[3,3,3,384,384]{4,3,2,1,0:T(8,128)(2,1)} %weight.1, f32[384]{0:T(512)} %bias_in.1), custom_call_target="tpu_custom_call" | custom-call | flops 8153726976 | bytes 11894784 | tf_op jit(solution)/shard_map/pallas_call | solution.py:230
  15.6 1.2 %shard_map.69 = (bf16[4,256,384]{2,1,0:T(8,128)(2,1)}, bf16[4,256,384]{2,1,0:T(8,128)(2,1)}) custom-call(f32[4,256,384]{2,1,0:T(8,128)S(1)} %get-tuple-element.5.acc, bf16[4,256,384]{2,1,0:T(8,128)(2,1)S(1)} %get-tuple-element.6.fresh, bf16[2,256,384]{2,1,0:T(8,128)(2,1)S(1)} %get-tuple-element.7.got), custom_call_target="tpu_custom_call" | custom-call | flops 393216 | bytes 3932160 | tf_op jit(solution)/shard_map/pallas_call | solution.py:262
